TPU v7x, 32 devices: a whole 2x2x4 slice. The times are simulated.
32 devices in a mesh: mat: 8 (over y, x, core), frac: 4 (over z).
Axes of the slice: x: 2, y: 2, z: 4, core: 2. Of those that a mesh axis runs over, the one named last changes fastest.
Arguments:
- pressure: float32 [256, 128, 256], P('mat', 'frac'), may hold values from -6 to 6
- source: float32 [256, 128, 256], P('mat', 'frac'), may hold values from -12 to 12
- storage: float32 [256, 128, 256], P('mat', 'frac'), may hold values from 0.25 to 2
- matrix_conc: float32 [256, 128, 256], P('mat', 'frac'), may hold values from -6 to 6
- frac_pressure: float32 [512, 128], P(('mat', 'frac')), may hold values from -6 to 6
- frac_conc: float32 [512, 128], P(('mat', 'frac')), may hold values from -6 to 6
- tile_blocks: bfloat16 [512, 8, 128, 128], P(('mat', 'frac')), may hold values from -0.5 to 0.5
- tile_links: int32 [512, 8], P(('mat', 'frac')), may hold values from 0 to 63
- tile_dir: int32 [512, 8], P(('mat', 'frac')), may hold values from 0 to 1
- link_cell: int32 [1024, 64], P(('mat', 'frac')), may hold values from 0 to 262143
- link_frac: int32 [1024, 64], P(('mat', 'frac')), may hold values from 0 to 2047
- link_trans: float32 [1024, 64], P(('mat', 'frac')), may hold values from 0.05 to 1
- link_count: int32 [1024], P(('mat', 'frac')), may hold values from 1 to 64
Outputs:
- smoothed: float32 [256, 128, 256], P('mat', 'frac')
- matrix_out: float32 [256, 128, 256], P('mat', 'frac')
- frac_out: float32 [512, 128], P(('mat', 'frac'))
Inputs may be any that keep to these rules, and one draw needn't show every extreme that they name: `tile_links`: indices among the 64 tiles of the devices that share the mat index.
All inputs are finite; a program needn't handle non-finite values.
Results may differ from a plain program's by a relative error of at most 0.00056.
Values may be sent and summed in bfloat16 or wider, within the bound.
A program may use at most 128 MiB of HBM per device.

v0:
```python
import functools

import jax
import jax.numpy as jnp
from jax import lax
from jax.experimental import pallas as pl
from jax.experimental.pallas import tpu as pltpu
from jax.sharding import PartitionSpec as P

OMEGA = 0.8
DT_FRAC = 0.1
DT_MATRIX = 0.5
MESH = pl.DeviceIdType.MESH
F32 = jnp.float32
BF16 = jnp.bfloat16
LANES = 128
NT = (((1,), (1,)), ((), ()))


def split(v):
    high = v.astype(BF16)
    return high, (v - high.astype(F32)).astype(BF16)


def kernel(
    nm, nf,
    pressure, source, storage, conc, blocks, frac_pressure, frac_conc, tile_links, tile_dir, cell, pack,
    out_s, out_m, out_f,
    pv, sv, rv, cv, fv, bv, yst, hx, hy, hot, ft, place, lhs, wt,
    conc_at, field_at, rets, rx0, rx1, rx2, group, xin, xout, inflow, outflow,
    load_sem, store_sem, halo_send, halo_recv, a2a_send, a2a_recv, group_send, group_recv,
):
    m, f = lax.axis_index("mat"), lax.axis_index("frac")
    peers = nm * nf
    rows = peers // 2
    me = m * nf + f
    nx, ny, nz = pv.shape
    zbits = nz.bit_length() - 1
    tiles, tsize = frac_conc.shape
    tbits = tsize.bit_length() - 1
    kk = bv.shape[1]
    cells = nx * ny

    loads = [
        pltpu.make_async_copy(a, b, load_sem.at[i])
        for i, (a, b) in enumerate(
            ((pressure, pv), (storage, sv), (source, rv), (conc, cv), (blocks, bv))
        )
    ]
    for copy in loads:
        copy.start()

    barrier = pltpu.get_barrier_semaphore()

    def greet(i, carry):
        dest = lax.rem(me + i, peers)
        pl.semaphore_signal(
            barrier, inc=1, device_id=(lax.div(dest, nf), lax.rem(dest, nf)), device_id_type=MESH
        )
        return carry

    lax.fori_loop(1, peers, greet, 0)

    @pl.when(m == 0)
    def _():
        for k in range(2):
            hx[k, 0] = jnp.zeros((ny, nz), F32)

    @pl.when(m == nm - 1)
    def _():
        for k in range(2):
            hx[k, 1] = jnp.zeros((ny, nz), F32)

    @pl.when(f == 0)
    def _():
        for k in range(2):
            hy[k, 0] = jnp.zeros((nx, nz), F32)

    @pl.when(f == nf - 1)
    def _():
        for k in range(2):
            hy[k, 1] = jnp.zeros((nx, nz), F32)

    group[f] = frac_conc[...].astype(BF16)

    loads[0].wait()

    def stage(x, carry):
        yst[0, 0, pl.ds(x, 1), :] = pv[x, 0:1, :]
        yst[0, 1, pl.ds(x, 1), :] = pv[x, ny - 1 : ny, :]
        return carry

    lax.fori_loop(0, nx, stage, 0)

    def halo(k, field):
        out = []
        for d, (src, dst, to, sends, gets) in enumerate((
            (field.at[0], hx.at[k, 1], (m - 1, f), m > 0, m < nm - 1),
            (field.at[nx - 1], hx.at[k, 0], (m + 1, f), m < nm - 1, m > 0),
            (yst.at[k, 0], hy.at[k, 1], (m, f - 1), f > 0, f < nf - 1),
            (yst.at[k, 1], hy.at[k, 0], (m, f + 1), f < nf - 1, f > 0),
        )):
            copy = pltpu.make_async_remote_copy(
                src_ref=src, dst_ref=dst, send_sem=halo_send.at[k, d], recv_sem=halo_recv.at[k, d],
                device_id=to, device_id_type=MESH,
            )
            out.append((copy, sends, gets))
        return out

    def start_halo(copies):
        for copy, sends, gets in copies:
            pl.when(sends)(copy.start)

    def wait_halo(copies):
        for copy, sends, gets in copies:
            pl.when(gets)(copy.wait_recv)
        for copy, sends, gets in copies:
            pl.when(sends)(copy.wait_send)

    def exchange(src, dst, k):
        def send(i, carry):
            dest = lax.rem(me + i, peers)
            pltpu.make_async_remote_copy(
                src_ref=src.at[lax.rem(dest, rows)], dst_ref=dst.at[me],
                send_sem=a2a_send.at[k], recv_sem=a2a_recv.at[k],
                device_id=(lax.div(dest, nf), lax.rem(dest, nf)), device_id_type=MESH,
            ).start()
            return carry

        lax.fori_loop(1, peers, send, 0)
        dst[me] = src[lax.rem(me, rows)]

    def wait_exchange(dst, k):
        part = dst.at[pl.ds(0, peers - 1)]
        pltpu.make_async_copy(part, part, a2a_recv.at[k]).wait()
        pltpu.make_async_copy(part, part, a2a_send.at[k]).wait()

    pl.semaphore_wait(barrier, peers - 1)
    first = halo(0, pv)
    start_halo(first)
    exchange(pack, rx0, 0)

    def spread(i, carry):
        pltpu.make_async_remote_copy(
            src_ref=group.at[f], dst_ref=group.at[f], send_sem=group_send, recv_sem=group_recv,
            device_id=(m, lax.rem(f + i, nf)), device_id_type=MESH,
        ).start()
        return carry

    lax.fori_loop(1, nf, spread, 0)

    upper = me >= rows
    lane = lax.broadcasted_iota(jnp.int32, (1, LANES), 1)
    left = lane < LANES // 2

    def joined(a, b):
        a = jnp.where(upper, pltpu.roll(a, LANES // 2, 1), a)
        b = jnp.where(upper, b, pltpu.roll(b, LANES // 2, 1))
        return jnp.where(left, a, b)

    def at(r):
        return pl.ds(pl.multiple_of(r * LANES, LANES), LANES)

    row_ids = lax.broadcasted_iota(jnp.int32, (cells, LANES), 0)

    def mark(r, carry):
        high = lax.shift_right_logical(cell[r], zbits)
        hot[:, at(r)] = jnp.where(row_ids == high, 1.0, 0.0).astype(BF16)
        return carry

    lax.fori_loop(0, rows, mark, 0)

    loads[1].wait()
    loads[2].wait()

    def factors(x, carry):
        scale = OMEGA / (6.0 + sv[x])
        sv[x] = scale
        rv[x] = rv[x] * scale
        return carry

    lax.fori_loop(0, nx, factors, 0)

    iy = lax.broadcasted_iota(jnp.int32, (ny, nz), 0)
    iz = lax.broadcasted_iota(jnp.int32, (ny, nz), 1)

    def sweep(src, dst, k, faces):
        def slab(x, carry):
            cur = src[x]
            before = jnp.where(x == 0, hx[k, 0], src[jnp.maximum(x - 1, 0)])
            after = jnp.where(x == nx - 1, hx[k, 1], src[jnp.minimum(x + 1, nx - 1)])
            beside = before + after
            beside += jnp.where(iy == 0, hy[k, 0, pl.ds(x, 1), :], pltpu.roll(cur, 1, 0))
            beside += jnp.where(iy == ny - 1, hy[k, 1, pl.ds(x, 1), :], pltpu.roll(cur, ny - 1, 0))
            beside += jnp.where(iz == 0, 0.0, pltpu.roll(cur, 1, 1))
            beside += jnp.where(iz == nz - 1, 0.0, pltpu.roll(cur, nz - 1, 1))
            new = (1.0 - OMEGA) * cur + (sv[x] * beside + rv[x])
            dst[x] = new
            if faces:
                yst[1, 0, pl.ds(x, 1), :] = new[0:1, :]
                yst[1, 1, pl.ds(x, 1), :] = new[ny - 1 : ny, :]
            return carry

        lax.fori_loop(0, nx, slab, 0)

    wait_halo(first)
    sweep(pv, fv, 0, True)
    second = halo(1, fv)
    start_halo(second)

    per = LANES // ny

    def turn(field):
        def body(c, carry):
            part = field[pl.ds(c * per, per)].reshape(LANES, nz)
            high, low = split(jnp.transpose(part))
            ft[0:nz, at(c)] = high
            ft[nz : 2 * nz, at(c)] = low
            return carry

        lax.fori_loop(0, cells // LANES, body, 0)

    place_ids = lax.broadcasted_iota(jnp.int32, (nz, LANES), 0)
    wide = 2

    def gather(dst, scaled):
        def body(c, carry):
            off = pl.multiple_of(c * (wide * LANES), wide * LANES)
            got = jnp.dot(ft[...], hot[:, pl.ds(off, wide * LANES)], preferred_element_type=F32)
            both = got[0:nz] + got[nz : 2 * nz]
            for j in range(wide):
                r = c * wide + j
                low = jnp.bitwise_and(cell[r], nz - 1)
                part = both[:, j * LANES : (j + 1) * LANES]
                value = jnp.sum(jnp.where(place_ids == low, part, 0.0), axis=0, keepdims=True)
                if scaled:
                    value = value * pack[r, 1:2, :]
                dst[r] = value
            return carry

        lax.fori_loop(0, rows // wide, body, 0)

    loads[3].wait()
    turn(cv)
    gather(conc_at, False)

    wait_halo(second)
    sweep(fv, pv, 1, False)
    store_s = pltpu.make_async_copy(pv, out_s, store_sem.at[0])
    store_s.start()
    turn(pv)
    gather(field_at, True)
    exchange(field_at, rx1, 1)

    got_group = group.at[pl.ds(0, nf - 1)]
    pltpu.make_async_copy(got_group, got_group, group_recv).wait()
    pltpu.make_async_copy(got_group, got_group, group_send).wait()
    count = nf * tiles
    inward = tile_dir[...] == 1
    tile_hot = jnp.where(
        (lax.broadcasted_iota(jnp.int32, (tiles * kk, count), 1) == tile_links[...]) & inward, 1.0, 0.0
    ).astype(BF16)
    picked = jnp.dot(tile_hot, group[...].reshape(count, tsize), preferred_element_type=F32)
    xin[...] = picked.reshape(tiles, kk, tsize)
    xout[...] = jnp.broadcast_to(jnp.where(tile_dir[...] == 0, 1.0, 0.0), (tiles * kk, tsize)).reshape(
        tiles, kk, tsize
    )
    loads[4].wait()
    sub = lax.broadcasted_iota(jnp.int32, (2 * kk, tsize), 0)

    def flow(t, carry):
        both = jnp.concatenate([xin[t], xout[t]], axis=0).astype(BF16)
        res = lax.dot_general(both, bv[t].reshape(kk * tsize, tsize), NT, preferred_element_type=F32)
        acc = jnp.zeros((2 * kk, tsize), F32)
        for k in range(kk):
            acc += jnp.where((sub == k) | (sub == k + kk), res[:, k * tsize : (k + 1) * tsize], 0.0)
        inflow[pl.ds(t, 1), :] = jnp.sum(acc[0:kk], axis=0, keepdims=True)
        outflow[pl.ds(t, 1), :] = jnp.sum(acc[kk : 2 * kk], axis=0, keepdims=True)
        return carry

    lax.fori_loop(0, tiles, flow, 0)

    wait_exchange(rx0, 0)
    tile_ids = lax.broadcasted_iota(jnp.int32, (tiles, LANES), 0)
    frac_ids = lax.broadcasted_iota(jnp.int32, (tsize, LANES), 0)

    def prepare(r, carry):
        ids = joined(rx0[r, 0:1, :], rx0[r + rows, 0:1, :]).astype(jnp.int32)
        place[:, at(r)] = jnp.where(frac_ids == jnp.bitwise_and(ids, tsize - 1), 1.0, 0.0).astype(BF16)
        here = tile_ids == lax.shift_right_logical(ids, tbits)
        trans = joined(rx0[r, 1:2, :], rx0[r + rows, 1:2, :])
        high, low = split(jnp.where(here, trans, 0.0))
        lhs[2 * tiles : 3 * tiles, at(r)] = high
        lhs[3 * tiles : 4 * tiles, at(r)] = low
        return carry

    lax.fori_loop(0, rows, prepare, 0)

    wait_exchange(rx1, 1)

    def carried(r, carry):
        ids = joined(rx0[r, 0:1, :], rx0[r + rows, 0:1, :]).astype(jnp.int32)
        here = tile_ids == lax.shift_right_logical(ids, tbits)
        value = joined(rx1[r], rx1[r + rows])
        high, low = split(jnp.where(here, value, 0.0))
        lhs[0:tiles, at(r)] = high
        lhs[tiles : 2 * tiles, at(r)] = low
        return carry

    lax.fori_loop(0, rows, carried, 0)
    sums = lax.dot_general(lhs[...], place[...], NT, preferred_element_type=F32)
    first_sum = sums[0:tiles] + sums[tiles : 2 * tiles]
    second_sum = sums[2 * tiles : 3 * tiles] + sums[3 * tiles : 4 * tiles]
    transfer = first_sum - frac_pressure[...] * second_sum
    new_frac = frac_conc[...] + DT_FRAC * (inflow[...] - outflow[...] * frac_conc[...] + transfer)
    out_f[...] = new_frac
    high, low = split(new_frac)
    parts = jnp.concatenate([high, low], axis=0)

    def give(r, carry):
        ids = joined(rx0[r, 0:1, :], rx0[r + rows, 0:1, :]).astype(jnp.int32)
        here = tile_ids == lax.shift_right_logical(ids, tbits)
        got = jnp.dot(parts, place[:, at(r)], preferred_element_type=F32)
        rets[r] = jnp.sum(
            jnp.where(here, got[0:tiles] + got[tiles : 2 * tiles], 0.0), axis=0, keepdims=True
        )
        return carry

    lax.fori_loop(0, rows, give, 0)
    exchange(rets, rx2, 2)
    wait_exchange(rx2, 2)

    def weigh(r, carry):
        back = joined(rx2[r], rx2[r + rows])
        term = DT_MATRIX * pack[r, 1:2, :] * (back - conc_at[r])
        low_ids = jnp.bitwise_and(cell[r], nz - 1)
        high, low = split(jnp.where(place_ids == low_ids, term, 0.0))
        wt[0:nz, at(r)] = high
        wt[nz : 2 * nz, at(r)] = low
        return carry

    lax.fori_loop(0, rows, weigh, 0)
    slabs = 8

    def add(c, carry):
        size = slabs * ny
        off = pl.multiple_of(c * size, size)
        got = lax.dot_general(hot[pl.ds(off, size), :], wt[...], NT, preferred_element_type=F32)
        change = (got[:, 0:nz] + got[:, nz : 2 * nz]).reshape(slabs, ny, nz)
        where = pl.ds(c * slabs, slabs)
        cv[where] = cv[where] + change
        return carry

    lax.fori_loop(0, nx // slabs, add, 0)
    store_m = pltpu.make_async_copy(cv, out_m, store_sem.at[1])
    store_m.start()
    store_m.wait()
    store_s.wait()


def on_device(
    nm, nf,
    pressure, source, storage, matrix_conc, frac_pressure, frac_conc, tile_blocks,
    tile_links, tile_dir, link_cell, link_frac, link_trans, link_count,
):
    block = pressure.shape
    nx, ny, nz = block
    tiles, tsize = frac_conc.shape
    kk = tile_links.shape[1]
    peers, slots = link_trans.shape
    rows = peers // 2
    links = peers * slots
    live = jnp.arange(slots, dtype=jnp.int32)[None, :] < link_count[:, None]
    live_trans = jnp.where(live, link_trans, 0.0)

    def paired(a):
        return jnp.concatenate([a[:rows], a[rows:]], axis=1)

    cell = paired(link_cell)[:, None, :]
    pack = jnp.stack([paired(link_frac).astype(F32), paired(live_trans)], axis=1)
    hbm = pl.BlockSpec(memory_space=pl.ANY)
    vmem = pl.BlockSpec(memory_space=pltpu.VMEM)
    field = pltpu.VMEM(block, F32)
    row = pltpu.VMEM((rows, 1, LANES), F32)
    dma = pltpu.SemaphoreType.DMA
    return pl.pallas_call(
        functools.partial(kernel, nm, nf),
        out_shape=(
            jax.ShapeDtypeStruct(block, F32),
            jax.ShapeDtypeStruct(block, F32),
            jax.ShapeDtypeStruct((tiles, tsize), F32),
        ),
        in_specs=[hbm] * 5 + [vmem] * 6,
        out_specs=(hbm, hbm, vmem),
        scratch_shapes=[
            field, field, field, field, field,
            pltpu.VMEM(tile_blocks.shape, BF16),
            pltpu.VMEM((2, 2, nx, nz), F32),
            pltpu.VMEM((2, 2, ny, nz), F32),
            pltpu.VMEM((2, 2, nx, nz), F32),
            pltpu.VMEM((nx * ny, links), BF16),
            pltpu.VMEM((2 * nz, nx * ny), BF16),
            pltpu.VMEM((tsize, links), BF16),
            pltpu.VMEM((4 * tiles, links), BF16),
            pltpu.VMEM((2 * nz, links), BF16),
            row, row, row,
            pltpu.VMEM((peers, 2, LANES), F32),
            pltpu.VMEM((peers, 1, LANES), F32),
            pltpu.VMEM((peers, 1, LANES), F32),
            pltpu.VMEM((nf, tiles, tsize), BF16),
            pltpu.VMEM((tiles, kk, tsize), F32),
            pltpu.VMEM((tiles, kk, tsize), F32),
            pltpu.VMEM((tiles, tsize), F32),
            pltpu.VMEM((tiles, tsize), F32),
            dma((5,)), dma((2,)), dma((2, 4)), dma((2, 4)), dma((3,)), dma((3,)), dma, dma,
        ],
        compiler_params=pltpu.CompilerParams(
            collective_id=0, has_side_effects=True, vmem_limit_bytes=56 * 1024 * 1024
        ),
    )(
        pressure, source, storage, matrix_conc, tile_blocks, frac_pressure, frac_conc,
        tile_links.reshape(-1, 1), tile_dir.reshape(-1, 1), cell, pack,
    )


def solution(mesh):
    grid = P("mat", "frac", None)
    own = P(("mat", "frac"), None)
    in_specs = (
        grid, grid, grid, grid, own, own, P(("mat", "frac"), None, None, None),
        own, own, own, own, own, P(("mat", "frac")),
    )
    return jax.shard_map(
        functools.partial(on_device, mesh.shape["mat"], mesh.shape["frac"]),
        mesh=mesh, in_specs=in_specs, out_specs=(grid, grid, own), check_vma=False,
    )
```

profile of v0, /device:TPU:0, one launch (start us, length us, event | category | flops | bytes accessed | tf_op | source)
XLA Modules:
  0.0 57.7 jit_solution(5392604716737151553)
XLA Ops:
  0.6 0.8 %copy.20 = s32[16,8]{1,0:T(8,128)S(1)} copy(s32[16,8]{0,1:T(8,128)} %param.20) | data formatting | bytes 1024 | tf_op args[7]
  1.4 0.8 %copy.21 = s32[16,8]{1,0:T(8,128)S(1)} copy(s32[16,8]{0,1:T(8,128)} %param.21) | data formatting | bytes 1024 | tf_op args[8]
  2.1 0.8 %fusion = f32[32,64]{1,0:T(8,128)S(1)} fusion(f32[32,64]{1,0:T(8,128)} %param.24, s32[32]{0:T(128)} %param.25), kind=kLoop, calls=%fused_computation.2 | loop fusion | flops 4096 | bytes 16512 | tf_op jit(solution)/shard_map/jit(_where)/select_n | solution.py:374
  2.9 0.1 pad_maximum_fusion.1
  3.0 0.7 %fusion.3 = (s32[16,64]{1,0:T(8,128)S(1)}, s32[16,64]{1,0:T(8,128)S(1)}) fusion(s32[32,64]{1,0:T(8,128)} %param.22), kind=kLoop, calls=%fused_computation.8 | loop fusion | bytes 16384 | tf_op jit(solution)/shard_map/slice | solution.py:377
  3.7 0.7 %pad_add_fusion = s32[16,128]{1,0:T(8,128)} fusion(s32[16,64]{1,0:T(8,128)S(1)} %get-tuple-element.8, s32[16,64]{1,0:T(8,128)S(1)} %get-tuple-element.7), kind=kLoop, calls=%fused_computation.3 | loop fusion | flops 2048 | bytes 16384 | tf_op jit(solution)/shard_map/concatenate | solution.py:377
  4.4 0.7 %fusion.1 = (s32[16,64]{1,0:T(8,128)S(1)}, s32[16,64]{1,0:T(8,128)S(1)}) fusion(s32[32,64]{1,0:T(8,128)} %param.23), kind=kLoop, calls=%fused_computation.6 | loop fusion | bytes 16384 | tf_op jit(solution)/shard_map/slice | solution.py:377
  5.1 0.1 add_convert_fusion
  5.2 0.6 %pad_maximum_fusion.pack = f32[16,2,128]{2,1,0:T(2,128)} fusion(f32[16,1,128]{2,1,0:T(1,128)S(1)} %bitcast.5, f32[16,1,128]{2,1,0:T(1,128)S(1)} %add_convert_fusion), kind=kLoop, calls=%fused_computation | loop fusion | flops 4096 | bytes 32768 | tf_op jit(solution)/shard_map/stack | solution.py:380
  5.8 0.7 %reshape.45.tile_dir = s32[128,1]{1,0:T(8,128)} reshape(s32[16,8]{1,0:T(8,128)S(1)} %copy.21) | data formatting | bytes 1024 | tf_op jit(solution)/shard_map/reshape | solution.py:422
  6.5 0.7 %reshape.44.tile_links = s32[128,1]{1,0:T(8,128)} reshape(s32[16,8]{1,0:T(8,128)S(1)} %copy.20) | data formatting | bytes 1024 | tf_op jit(solution)/shard_map/reshape | solution.py:422
  7.3 45.2 %shard_map.148 = (f32[32,32,256]{2,1,0:T(8,128)}, f32[32,32,256]{2,1,0:T(8,128)}, f32[16,128]{1,0:T(8,128)}) custom-call(f32[32,32,256]{2,1,0:T(8,128)} %pressure.1, f32[32,32,256]{2,1,0:T(8,128)} %source.1, f32[32,32,256]{2,1,0:T(8,128)} %storage.1, f32[32,32,256]{2,1,0:T(8,128)} %conc.1, bf16[16,8,128,128]{3,2,1,0:T(8,128)(2,1)} %blocks.1, ...), custom_call_target="tpu_custom_call" | custom-call | tf_op jit(solution)/shard_map/pallas_call | solution.py:386
  52.5 0.0 copy-start
  52.5 2.3 %copy.27 = f32[32,32,256]{2,1,0:T(8,128)} copy(f32[32,32,256]{2,1,0:T(8,128)} %get-tuple-element.12) | data formatting | bytes 2097152
  54.8 2.3 %copy.28 = f32[32,32,256]{2,1,0:T(8,128)} copy(f32[32,32,256]{2,1,0:T(8,128)} %get-tuple-element.13) | data formatting | bytes 2097152
  57.1 0.0 copy-done
  57.1 0.6 %copy.29 = f32[16,128]{1,0:T(8,128)} copy(f32[16,128]{1,0:T(8,128)S(1)} %copy-done) | data formatting | bytes 16384
  (1 shorter events, 0.0 us)
Async XLA Ops:
  52.5 4.6 %copy-start = (f32[16,128]{1,0:T(8,128)S(1)}, f32[16,128]{1,0:T(8,128)}, u32[]{:S(2)}) copy-start(f32[16,128]{1,0:T(8,128)} %get-tuple-element.14) | copy-start | bytes 24580
where the time goes:
time: 58.3 us; the launch traced here: 57.7 us
  Pallas kernels  45.2 us (78%)
  local copies, waits for them, and re-layouts  9.6 us (16%)
  other arithmetic  2.24 us (4%)
  between operations  0.66 us (1%)
    pallas_call x1, Pallas kernels, on_device(): pl.pallas_call(functools.partial(kernel, nm, nf), out_shape=(jax.ShapeDty...  45.2 us
    unnamed x7, local copies, waits for them, and re-layouts  6.74 us
    slice x3, local copies, waits for them, and re-layouts, paired(): return jnp.concatenate([a[:rows], a[rows:]], axis=1)  1.44 us

commit v1 on v0

--- a/solution.py
+++ b/solution.py
@@ -24,9 +24,9 @@
 
 def kernel(
     nm, nf,
-    pressure, source, storage, conc, blocks, frac_pressure, frac_conc, tile_links, tile_dir, cell, pack,
+    pressure, source, storage, conc, blocks, frac_pressure, frac_conc, tile_links, tile_dir, link_cell, link_frac, link_trans, link_count,
     out_s, out_m, out_f,
-    pv, sv, rv, cv, fv, bv, yst, hx, hy, hot, ft, place, lhs, wt,
+    pv, sv, rv, cv, fv, bv, cell, frac_rows, trans_rows, pack, tile_hot, yst, hx, hy, hot, ft, place, lhs, wt,
     conc_at, field_at, rets, rx0, rx1, rx2, group, xin, xout, inflow, outflow,
     load_sem, store_sem, halo_send, halo_recv, a2a_send, a2a_recv, group_send, group_recv,
 ):
@@ -82,6 +82,24 @@
             hy[k, 1] = jnp.zeros((nx, nz), F32)
 
     group[f] = frac_conc[...].astype(BF16)
+    lane = lax.broadcasted_iota(jnp.int32, (1, LANES), 1)
+    slots = LANES // 2
+    left = lane < slots
+
+    def paired(ref):
+        return jnp.concatenate([ref[0:rows, :], ref[rows : 2 * rows, :]], axis=1)
+
+    cell[...] = paired(link_cell)
+    frac_rows[...] = paired(link_frac).astype(F32)
+    trans_rows[...] = paired(link_trans)
+
+    def fill(r, carry):
+        bound = jnp.where(left, link_count[r], link_count[r + rows] + slots)
+        pack[r, 0:1, :] = frac_rows[pl.ds(r, 1), :]
+        pack[r, 1:2, :] = jnp.where(lane < bound, trans_rows[pl.ds(r, 1), :], 0.0)
+        return carry
+
+    lax.fori_loop(0, rows, fill, 0)
 
     loads[0].wait()
 
@@ -150,8 +168,6 @@
     lax.fori_loop(1, nf, spread, 0)
 
     upper = me >= rows
-    lane = lax.broadcasted_iota(jnp.int32, (1, LANES), 1)
-    left = lane < LANES // 2
 
     def joined(a, b):
         a = jnp.where(upper, pltpu.roll(a, LANES // 2, 1), a)
@@ -164,7 +180,7 @@
     row_ids = lax.broadcasted_iota(jnp.int32, (cells, LANES), 0)
 
     def mark(r, carry):
-        high = lax.shift_right_logical(cell[r], zbits)
+        high = lax.shift_right_logical(cell[pl.ds(r, 1), :], zbits)
         hot[:, at(r)] = jnp.where(row_ids == high, 1.0, 0.0).astype(BF16)
         return carry
 
@@ -201,7 +217,7 @@
                 yst[1, 1, pl.ds(x, 1), :] = new[ny - 1 : ny, :]
             return carry
 
-        lax.fori_loop(0, nx, slab, 0)
+        lax.fori_loop(0, nx, slab, 0, unroll=2)
 
     wait_halo(first)
     sweep(pv, fv, 0, True)
@@ -230,7 +246,7 @@
             both = got[0:nz] + got[nz : 2 * nz]
             for j in range(wide):
                 r = c * wide + j
-                low = jnp.bitwise_and(cell[r], nz - 1)
+                low = jnp.bitwise_and(cell[pl.ds(r, 1), :], nz - 1)
                 part = both[:, j * LANES : (j + 1) * LANES]
                 value = jnp.sum(jnp.where(place_ids == low, part, 0.0), axis=0, keepdims=True)
                 if scaled:
@@ -256,15 +272,16 @@
     pltpu.make_async_copy(got_group, got_group, group_recv).wait()
     pltpu.make_async_copy(got_group, got_group, group_send).wait()
     count = nf * tiles
-    inward = tile_dir[...] == 1
-    tile_hot = jnp.where(
-        (lax.broadcasted_iota(jnp.int32, (tiles * kk, count), 1) == tile_links[...]) & inward, 1.0, 0.0
-    ).astype(BF16)
-    picked = jnp.dot(tile_hot, group[...].reshape(count, tsize), preferred_element_type=F32)
+    tile_no = lax.broadcasted_iota(jnp.int32, (kk, count), 1)
+    for t in range(tiles):
+        inward = tile_dir[:, t : t + 1] == 1
+        chosen = (tile_no == tile_links[:, t : t + 1]) & inward
+        tile_hot[t * kk : (t + 1) * kk, :] = jnp.where(chosen, 1.0, 0.0)
+        xout[t] = jnp.broadcast_to(jnp.where(inward, 0.0, 1.0), (kk, tsize))
+    picked = jnp.dot(
+        tile_hot[...].astype(BF16), group[...].reshape(count, tsize), preferred_element_type=F32
+    )
     xin[...] = picked.reshape(tiles, kk, tsize)
-    xout[...] = jnp.broadcast_to(jnp.where(tile_dir[...] == 0, 1.0, 0.0), (tiles * kk, tsize)).reshape(
-        tiles, kk, tsize
-    )
     loads[4].wait()
     sub = lax.broadcasted_iota(jnp.int32, (2 * kk, tsize), 0)
 
@@ -294,7 +311,7 @@
         lhs[3 * tiles : 4 * tiles, at(r)] = low
         return carry
 
-    lax.fori_loop(0, rows, prepare, 0)
+    lax.fori_loop(0, rows, prepare, 0, unroll=4)
 
     wait_exchange(rx1, 1)
 
@@ -307,7 +324,7 @@
         lhs[tiles : 2 * tiles, at(r)] = low
         return carry
 
-    lax.fori_loop(0, rows, carried, 0)
+    lax.fori_loop(0, rows, carried, 0, unroll=4)
     sums = lax.dot_general(lhs[...], place[...], NT, preferred_element_type=F32)
     first_sum = sums[0:tiles] + sums[tiles : 2 * tiles]
     second_sum = sums[2 * tiles : 3 * tiles] + sums[3 * tiles : 4 * tiles]
@@ -326,20 +343,20 @@
         )
         return carry
 
-    lax.fori_loop(0, rows, give, 0)
+    lax.fori_loop(0, rows, give, 0, unroll=4)
     exchange(rets, rx2, 2)
     wait_exchange(rx2, 2)
 
     def weigh(r, carry):
         back = joined(rx2[r], rx2[r + rows])
         term = DT_MATRIX * pack[r, 1:2, :] * (back - conc_at[r])
-        low_ids = jnp.bitwise_and(cell[r], nz - 1)
+        low_ids = jnp.bitwise_and(cell[pl.ds(r, 1), :], nz - 1)
         high, low = split(jnp.where(place_ids == low_ids, term, 0.0))
         wt[0:nz, at(r)] = high
         wt[nz : 2 * nz, at(r)] = low
         return carry
 
-    lax.fori_loop(0, rows, weigh, 0)
+    lax.fori_loop(0, rows, weigh, 0, unroll=2)
     slabs = 8
 
     def add(c, carry):
@@ -370,16 +387,10 @@
     peers, slots = link_trans.shape
     rows = peers // 2
     links = peers * slots
-    live = jnp.arange(slots, dtype=jnp.int32)[None, :] < link_count[:, None]
-    live_trans = jnp.where(live, link_trans, 0.0)
-
-    def paired(a):
-        return jnp.concatenate([a[:rows], a[rows:]], axis=1)
-
-    cell = paired(link_cell)[:, None, :]
-    pack = jnp.stack([paired(link_frac).astype(F32), paired(live_trans)], axis=1)
-    hbm = pl.BlockSpec(memory_space=pl.ANY)
+    hbm = pl.BlockSpec(memory_space=pltpu.HBM)
+    free = pl.BlockSpec(memory_space=pl.ANY)
     vmem = pl.BlockSpec(memory_space=pltpu.VMEM)
+    smem = pl.BlockSpec(memory_space=pltpu.SMEM)
     field = pltpu.VMEM(block, F32)
     row = pltpu.VMEM((rows, 1, LANES), F32)
     dma = pltpu.SemaphoreType.DMA
@@ -390,11 +401,16 @@
             jax.ShapeDtypeStruct(block, F32),
             jax.ShapeDtypeStruct((tiles, tsize), F32),
         ),
-        in_specs=[hbm] * 5 + [vmem] * 6,
-        out_specs=(hbm, hbm, vmem),
+        in_specs=[hbm] * 5 + [vmem] * 7 + [smem],
+        out_specs=(free, free, vmem),
         scratch_shapes=[
             field, field, field, field, field,
             pltpu.VMEM(tile_blocks.shape, BF16),
+            pltpu.VMEM((rows, LANES), jnp.int32),
+            pltpu.VMEM((rows, LANES), F32),
+            pltpu.VMEM((rows, LANES), F32),
+            pltpu.VMEM((rows, 2, LANES), F32),
+            pltpu.VMEM((tiles * kk, nf * tiles), F32),
             pltpu.VMEM((2, 2, nx, nz), F32),
             pltpu.VMEM((2, 2, ny, nz), F32),
             pltpu.VMEM((2, 2, nx, nz), F32),
@@ -419,7 +435,7 @@
         ),
     )(
         pressure, source, storage, matrix_conc, tile_blocks, frac_pressure, frac_conc,
-        tile_links.reshape(-1, 1), tile_dir.reshape(-1, 1), cell, pack,
+        tile_links.T, tile_dir.T, link_cell, link_frac, link_trans, link_count,
     )
 
 

time: 58.3 us -> 45.9 us (0.79)
  Pallas kernels: 45.2 us -> 39.8 us
  local copies, waits for them, and re-layouts: 9.6 us -> 5.22 us
  other arithmetic: 2.24 us -> 0 us
    pallas_call x1, Pallas kernels: 45.2 us -> 39.8 us  [on_device(): pl.pallas_call(functools.partial(kernel, nm, nf), out_shape=(jax.ShapeDty...]
    unnamed x7 -> x5, local copies, waits for them, and re-layouts: 6.74 us -> 5.22 us
    slice x3 -> x0, local copies, waits for them, and re-layouts: 1.44 us -> none  [paired(): return jnp.concatenate([a[:rows], a[rows:]], axis=1)]
    reshape x2 -> x0, local copies, waits for them, and re-layouts: 1.42 us -> none  [the longest x1 0.71 us: on_device(): tile_links.reshape(-1, 1)]
    select_n x1 -> x0, other arithmetic: 0.79 us -> none  [on_device(): live_trans = jnp.where(live, link_trans, 0.0)]
    concatenate x2 -> x0, other arithmetic: 0.75 us -> none  [paired(): return jnp.concatenate([a[:rows], a[rows:]], axis=1)]
    another operation x1 -> x0, other arithmetic: 0.62 us -> none  [on_device(): jnp.stack([paired(link_frac).astype(F32), paired(live_trans)], axis=1)]
where the time goes in v1:
time: 45.9 us; the launch traced here: 45.7 us
  Pallas kernels  39.8 us (87%)
  local copies, waits for them, and re-layouts  5.22 us (11%)
  between operations  0.65 us (1%)
    pallas_call x1, Pallas kernels, on_device(): pl.pallas_call(functools.partial(kernel, nm, nf), out_shape=(jax.ShapeDty...  39.8 us
    unnamed x5, local copies, waits for them, and re-layouts  5.22 us

profile of v1, /device:TPU:0, one launch (start us, length us, event | category | flops | bytes accessed | tf_op | source)
XLA Modules:
  0.0 45.7 jit_solution(10935076166561344156)
XLA Ops:
  0.6 39.8 %shard_map.148 = (f32[32,32,256]{2,1,0:T(8,128)}, f32[32,32,256]{2,1,0:T(8,128)}, f32[16,128]{1,0:T(8,128)}) custom-call(f32[32,32,256]{2,1,0:T(8,128)} %pressure.1, f32[32,32,256]{2,1,0:T(8,128)} %source.1, f32[32,32,256]{2,1,0:T(8,128)} %storage.1, f32[32,32,256]{2,1,0:T(8,128)} %conc.1, bf16[16,8,128,128]{3,2,1,0:T(8,128)(2,1)} %blocks.1, ...), custom_call_target="tpu_custom_call" | custom-call | tf_op jit(solution)/shard_map/pallas_call | solution.py:397
  40.4 0.0 copy-start
  40.5 2.3 %copy.19 = f32[32,32,256]{2,1,0:T(8,128)} copy(f32[32,32,256]{2,1,0:T(8,128)} %get-tuple-element.6) | data formatting | bytes 2097152
  42.8 2.3 %copy.20 = f32[32,32,256]{2,1,0:T(8,128)} copy(f32[32,32,256]{2,1,0:T(8,128)} %get-tuple-element.7) | data formatting | bytes 2097152
  45.1 0.0 copy-done
  45.1 0.6 %copy.21 = f32[16,128]{1,0:T(8,128)} copy(f32[16,128]{1,0:T(8,128)S(1)} %copy-done) | data formatting | bytes 16384
Async XLA Ops:
  40.4 4.6 %copy-start = (f32[16,128]{1,0:T(8,128)S(1)}, f32[16,128]{1,0:T(8,128)}, u32[]{:S(2)}) copy-start(f32[16,128]{1,0:T(8,128)} %get-tuple-element.8) | copy-start | bytes 24580
